TPU v7x, 512 devices: a whole 4x4x16 slice. The times are simulated.
512 devices in a mesh: seq: 32 (over z, core), blk: 16 (over x, y).
Axes of the slice: x: 4, y: 4, z: 16, core: 2. Of those that a mesh axis runs over, the one named last changes fastest.
Arguments:
- query: bfloat16 [65536, 4096], P(('seq', 'blk')), may hold values from -12 to 12
- key: bfloat16 [65536, 4096], P(('seq', 'blk')), may hold values from -80 to 80
- value: bfloat16 [65536, 4096], P(('seq', 'blk')), may hold values from -6 to 6
- recompute_index: int32 [3072], P(('seq', 'blk')), may hold values from 0 to 127, as said below
- counts: int32 [512], P(('seq', 'blk')), may hold values from 1 to 6, as said below
- timestep: int32 [1], replicated, may hold values from 0 to 49
- gate_table: float32 [50, 4096], replicated, may hold values from 0.5 to 2
Outputs:
- gated: bfloat16 [3072, 4096], P(('seq', 'blk'))
Inputs may be any that keep to these rules, and one draw needn't show every extreme that they name: `recompute_index`: the 6 positions of one device are distinct. `counts`: some device has all 6 slots live.
All inputs are finite; a program needn't handle non-finite values.
Results may differ from a plain program's by a relative error of at most 0.012.
Values may be sent and summed in bfloat16 or wider, within the bound.
No kernel may reach another device: no remote copies, remote signals or barrier semaphores. Data moves between devices by JAX's collectives and lax.ppermute only.
A program may use at most 64 MiB of HBM per device.

v0:
```python
import math
import jax
import jax.numpy as jnp
from jax import lax
from jax.sharding import PartitionSpec as P

HD = 128
HEADS = 32


def row_block(total):
    size = min(total, 512)
    while total % size != 0:
        size = size - 1
    return size


def partial_attention(queries, keys, values):
    total_rows, heads, depth = queries.shape
    size = row_block(total_rows)
    scale = 1.0 / math.sqrt(depth)

    def one_block(block):
        scores = jnp.einsum("rhd,khd->hrk", block, keys, preferred_element_type=jnp.float32) * scale
        top = jnp.max(scores, axis=2)
        powers = jnp.exp(scores - top[..., None])
        total = jnp.sum(powers, axis=2)
        mixed = jnp.einsum(
            "hrk,khd->rhd", powers.astype(jnp.bfloat16), values, preferred_element_type=jnp.float32
        )
        mixed = (mixed / total.T[..., None]).astype(jnp.bfloat16)
        return (mixed, top.T, total.T)

    blocks = queries.reshape(total_rows // size, size, heads, depth)
    mixed, top, total = lax.map(one_block, blocks)
    return (
        mixed.reshape(total_rows, heads, depth),
        top.reshape(total_rows, heads),
        total.reshape(total_rows, heads),
    )


def combine_parts(mixed, top, total):
    peak = jnp.max(top, axis=0)
    factor = total * jnp.exp(top - peak)
    summed = jnp.sum(factor[..., None] * mixed.astype(jnp.float32), axis=0)
    return (summed / jnp.sum(factor, axis=0)[..., None]).astype(jnp.bfloat16)


def local(query, key, value, recompute_index, counts, timestep, gate_table):
    seq_size = lax.axis_size("seq")
    blk_size = lax.axis_size("blk")
    slots = recompute_index.shape[0]
    width = query.shape[1]
    per_dev = HEADS // seq_size
    head_width = per_dev * HD
    chosen = query[recompute_index]
    keys, values = (
        lax.all_to_all(key, "seq", split_axis=1, concat_axis=0, tiled=True),
        lax.all_to_all(value, "seq", split_axis=1, concat_axis=0, tiled=True),
    )
    keys = keys.reshape(-1, per_dev, HD)
    values = values.reshape(-1, per_dev, HD)
    gathered = lax.all_gather(chosen, "blk", axis=0, tiled=True)
    spread = lax.all_to_all(gathered, "seq", split_axis=1, concat_axis=0, tiled=True)
    queries = spread.reshape(seq_size, blk_size, slots, head_width).transpose(1, 0, 2, 3)
    queries = queries.reshape(-1, per_dev, HD)
    mixed, top, total = partial_attention(queries, keys, values)
    mixed = mixed.reshape(blk_size, seq_size, slots, head_width)
    top = top.reshape(blk_size, seq_size, slots, per_dev)
    total = total.reshape(blk_size, seq_size, slots, per_dev)
    mixed = lax.all_to_all(
        lax.all_to_all(mixed, "seq", split_axis=1, concat_axis=3, tiled=True),
        "blk",
        split_axis=0,
        concat_axis=0,
        tiled=True,
    )
    top, total = (
        lax.all_to_all(
            lax.all_to_all(top, "seq", split_axis=1, concat_axis=3, tiled=True),
            "blk",
            split_axis=0,
            concat_axis=0,
            tiled=True,
        ),
        lax.all_to_all(
            lax.all_to_all(total, "seq", split_axis=1, concat_axis=3, tiled=True),
            "blk",
            split_axis=0,
            concat_axis=0,
            tiled=True,
        ),
    )
    attention = combine_parts(
        mixed.reshape(blk_size, slots, HEADS, HD),
        top.reshape(blk_size, slots, HEADS),
        total.reshape(blk_size, slots, HEADS),
    )
    attention = attention.reshape(slots, width)
    gate = lax.dynamic_index_in_dim(gate_table, timestep[0], 0, keepdims=False)
    gated = (gate[None, :] * attention.astype(jnp.float32)).astype(jnp.bfloat16)
    live = jnp.arange(slots, dtype=jnp.int32) < counts[0]
    return jnp.where(live[:, None], gated, jnp.zeros_like(gated))


def solution(mesh):
    in_specs = (
        P(("seq", "blk"), None),
        P(("seq", "blk"), None),
        P(("seq", "blk"), None),
        P(("seq", "blk")),
        P(("seq", "blk")),
        P(),
        P(),
    )
    out_specs = P(("seq", "blk"), None)
    return jax.shard_map(local, mesh=mesh, in_specs=in_specs, out_specs=out_specs, check_vma=False)
```

profile of v0, /device:TPU:8, one launch (start us, length us, event | category | flops | bytes accessed | tf_op | source)
XLA Modules:
  0.0 383.6 jit_solution(7330141485515167448)
XLA Ops:
  1.8 27.6 %all-gather.1 = bf16[16,6,4096]{2,1,0:T(8,128)(2,1)S(1)} all-gather(bf16[1,6,4096]{2,1,0:T(8,128)(2,1)S(1)} %bitcast.127), channel_id=2, replica_groups=mesh['seq'=32,'blk'=16] {'blk'}, dimensions={0}, use_global_device_ids=true | all-gather | bytes 835584 | tf_op jit(solution)/shard_map/all_gather | solution.py:64
  31.5 12.5 %all-to-all-start = ((bf16[96,32,128]{2,0,1:T(8,128)(2,1)}), bf16[96,32,128]{2,0,1:T(8,128)(2,1)S(1)}, u32[]{:S(2)}, u32[]{:S(2)}) async-start(bf16[96,32,128]{2,0,1:T(8,128)(2,1)} %copy.40), calls=%async_computation | async-start | bytes 1572864 | tf_op jit(solution)/shard_map/all_to_all | solution.py:65
  44.1 2.3 copy.43
  46.4 42.6 %all-to-all-done = bf16[96,32,128]{2,0,1:T(8,128)(2,1)S(1)} async-done(((bf16[96,32,128]{2,0,1:T(8,128)(2,1)}), bf16[96,32,128]{2,0,1:T(8,128)(2,1)S(1)}, u32[]{:S(2)}, u32[]{:S(2)}) %all-to-all-start) | async-done | bytes 786464 | tf_op jit(solution)/shard_map/all_to_all | solution.py:65
  89.0 3.9 %all-to-all-start.1 = ((bf16[128,32,128]{0,2,1:T(8,128)(2,1)}), bf16[128,32,128]{0,2,1:T(8,128)(2,1)S(1)}, u32[]{:S(2)}, u32[]{:S(2)}) async-start(bf16[128,32,128]{0,2,1:T(8,128)(2,1)} %bitcast.17), calls=%async_computation.1 | async-start | bytes 2097152 | tf_op jit(solution)/shard_map/all_to_all | solution.py:59
  93.0 2.3 copy.45
  95.2 54.2 %all-to-all-done.1 = bf16[128,32,128]{0,2,1:T(8,128)(2,1)S(1)} async-done(((bf16[128,32,128]{0,2,1:T(8,128)(2,1)}), bf16[128,32,128]{0,2,1:T(8,128)(2,1)S(1)}, u32[]{:S(2)}, u32[]{:S(2)}) %all-to-all-start.1) | async-done | bytes 1048608 | tf_op jit(solution)/shard_map/all_to_all | solution.py:59
  149.5 4.7 %all-to-all-start.2 = ((bf16[128,32,128]{0,2,1:T(8,128)(2,1)}), bf16[128,32,128]{0,2,1:T(8,128)(2,1)}, u32[]{:S(2)}, u32[]{:S(2)}) async-start(bf16[128,32,128]{0,2,1:T(8,128)(2,1)} %bitcast.20), calls=%async_computation.2 | async-start | bytes 2097152 | tf_op jit(solution)/shard_map/all_to_all | solution.py:60
  156.7 53.9 %all-to-all-done.2 = bf16[128,32,128]{0,2,1:T(8,128)(2,1)} async-done(((bf16[128,32,128]{0,2,1:T(8,128)(2,1)}), bf16[128,32,128]{0,2,1:T(8,128)(2,1)}, u32[]{:S(2)}, u32[]{:S(2)}) %all-to-all-start.2) | async-done | bytes 1048608 | tf_op jit(solution)/shard_map/all_to_all | solution.py:60
  212.2 35.4 %while.14 = (s32[]{:T(128)}, bf16[6,512,1,128]{3,1,2,0:T(8,128)(2,1)}, f32[6,512,1]{1,2,0:T(1,128)S(1)}, f32[6,512,1]{1,2,0:T(1,128)S(1)}, bf16[6,512,1,128]{3,1...) while((s32[]{:T(128)}, ...), condition=%wide.region_3.4_spmd, body=%wide.region_0.3_spmd.sunk | while | flops 1090649088 | bytes 27544664 | solution.py:35
  212.2 2.2 multiply_reduce_fusion.3
  248.8 3.9 %all-to-all-start.5 = ((f32[16,32,6,1]{0,3,2,1:T(1,128)}), f32[16,32,6,1]{0,3,2,1:T(1,128)S(1)}, u32[]{:S(2)}, u32[]{:S(2)}) async-start(f32[16,32,6,1]{0,3,2,1:T(1,128)} %copy.52), calls=%async_computation.5 | async-start | bytes 196608 | tf_op jit(solution)/shard_map/all_to_all | solution.py:81
  253.8 14.6 %all-to-all-done.5 = f32[16,32,6,1]{0,3,2,1:T(1,128)S(1)} async-done(((f32[16,32,6,1]{0,3,2,1:T(1,128)}), f32[16,32,6,1]{0,3,2,1:T(1,128)S(1)}, u32[]{:S(2)}, u32[]{:S(2)}) %all-to-all-start.5) | async-done | bytes 12320 | tf_op jit(solution)/shard_map/all_to_all | solution.py:81
  268.4 3.9 %all-to-all-start.3 = ((f32[16,32,6,1]{0,3,2,1:T(1,128)}), f32[16,32,6,1]{0,3,2,1:T(1,128)S(1)}, u32[]{:S(2)}, u32[]{:S(2)}) async-start(f32[16,32,6,1]{0,3,2,1:T(1,128)} %copy.48), calls=%async_computation.3 | async-start | bytes 196608 | tf_op jit(solution)/shard_map/all_to_all | solution.py:88
  274.5 13.6 %all-to-all-done.3 = f32[16,32,6,1]{0,3,2,1:T(1,128)S(1)} async-done(((f32[16,32,6,1]{0,3,2,1:T(1,128)}), f32[16,32,6,1]{0,3,2,1:T(1,128)S(1)}, u32[]{:S(2)}, u32[]{:S(2)}) %all-to-all-start.3) | async-done | bytes 12320 | tf_op jit(solution)/shard_map/all_to_all | solution.py:88
  288.0 5.7 %all-to-all-start.6 = ((f32[16,1,192]{2,1,0:T(1,128)}), f32[16,1,192]{2,1,0:T(1,128)S(1)}, u32[]{:S(2)}, u32[]{:S(2)}) async-start(f32[16,1,192]{2,1,0:T(1,128)} %reshape.106), calls=%async_computation.6 | async-start | bytes 32768 | tf_op jit(solution)/shard_map/all_to_all | solution.py:80
  296.8 3.1 all-to-all-done.6
  300.0 3.9 %all-to-all-start.7 = ((bf16[16,32,6,128]{3,0,2,1:T(8,128)(2,1)}), bf16[16,32,6,128]{3,0,2,1:T(8,128)(2,1)S(1)}, u32[]{:S(2)}, u32[]{:S(2)}) async-start(bf16[16,32,6,128]{3,0,2,1:T(8,128)(2,1)} %copy.56), calls=%async_computation.7 | async-start | bytes 1572864 | tf_op jit(solution)/shard_map/all_to_all | solution.py:73
  305.5 43.6 %all-to-all-done.7 = bf16[16,32,6,128]{3,0,2,1:T(8,128)(2,1)S(1)} async-done(((bf16[16,32,6,128]{3,0,2,1:T(8,128)(2,1)}), bf16[16,32,6,128]{3,0,2,1:T(8,128)(2,1)S(1)}, u32[]{:S(2)}, u32[]{:S(2)}) %all-to-all-start.7) | async-done | bytes 786464 | tf_op jit(solution)/shard_map/all_to_all | solution.py:73
  349.1 4.7 %all-to-all-start.4 = ((f32[16,1,192]{2,1,0:T(1,128)}), f32[16,1,192]{2,1,0:T(1,128)S(1)}, u32[]{:S(2)}, u32[]{:S(2)}) async-start(f32[16,1,192]{2,1,0:T(1,128)} %reshape.108), calls=%async_computation.4 | async-start | bytes 32768 | tf_op jit(solution)/shard_map/all_to_all | solution.py:87
  356.7 3.5 all-to-all-done.4
  360.2 5.5 %all-to-all-start.8 = ((bf16[16,1,6,4096]{3,2,1,0:T(8,128)(2,1)}), bf16[16,1,6,4096]{3,2,1,0:T(8,128)(2,1)}, u32[]{:S(2)}, u32[]{:S(2)}) async-start(bf16[16,1,6,4096]{3,2,1,0:T(8,128)(2,1)} %reshape.103), calls=%async_computation.8 | async-start | bytes 2097152 | tf_op jit(solution)/shard_map/all_to_all | solution.py:72
  371.0 9.5 %all-to-all-done.8 = bf16[16,1,6,4096]{3,2,1,0:T(8,128)(2,1)} async-done(((bf16[16,1,6,4096]{3,2,1,0:T(8,128)(2,1)}), bf16[16,1,6,4096]{3,2,1,0:T(8,128)(2,1)}, u32[]{:S(2)}, u32[]{:S(2)}) %all-to-all-start.8) | async-done | bytes 786464 | tf_op jit(solution)/shard_map/all_to_all | solution.py:72
  380.5 2.4 multiply_reduce_fusion.1
  (69 shorter events, 57.7 us)
Async XLA Ops:
  0.0 1.2 copy-start
  31.5 57.5 %all-to-all-start = ((bf16[96,32,128]{2,0,1:T(8,128)(2,1)}), bf16[96,32,128]{2,0,1:T(8,128)(2,1)S(1)}, u32[]{:S(2)}, u32[]{:S(2)}) async-start(bf16[96,32,128]{2,0,1:T(8,128)(2,1)} %copy.40), calls=%async_computation | async-start | bytes 1572864 | tf_op jit(solution)/shard_map/all_to_all | solution.py:65
  89.0 60.4 %all-to-all-start.1 = ((bf16[128,32,128]{0,2,1:T(8,128)(2,1)}), bf16[128,32,128]{0,2,1:T(8,128)(2,1)S(1)}, u32[]{:S(2)}, u32[]{:S(2)}) async-start(bf16[128,32,128]{0,2,1:T(8,128)(2,1)} %bitcast.17), calls=%async_computation.1 | async-start | bytes 2097152 | tf_op jit(solution)/shard_map/all_to_all | solution.py:59
  149.5 61.1 %all-to-all-start.2 = ((bf16[128,32,128]{0,2,1:T(8,128)(2,1)}), bf16[128,32,128]{0,2,1:T(8,128)(2,1)}, u32[]{:S(2)}, u32[]{:S(2)}) async-start(bf16[128,32,128]{0,2,1:T(8,128)(2,1)} %bitcast.20), calls=%async_computation.2 | async-start | bytes 2097152 | tf_op jit(solution)/shard_map/all_to_all | solution.py:60
  248.8 19.6 %all-to-all-start.5 = ((f32[16,32,6,1]{0,3,2,1:T(1,128)}), f32[16,32,6,1]{0,3,2,1:T(1,128)S(1)}, u32[]{:S(2)}, u32[]{:S(2)}) async-start(f32[16,32,6,1]{0,3,2,1:T(1,128)} %copy.52), calls=%async_computation.5 | async-start | bytes 196608 | tf_op jit(solution)/shard_map/all_to_all | solution.py:81
  268.4 19.6 %all-to-all-start.3 = ((f32[16,32,6,1]{0,3,2,1:T(1,128)}), f32[16,32,6,1]{0,3,2,1:T(1,128)S(1)}, u32[]{:S(2)}, u32[]{:S(2)}) async-start(f32[16,32,6,1]{0,3,2,1:T(1,128)} %copy.48), calls=%async_computation.3 | async-start | bytes 196608 | tf_op jit(solution)/shard_map/all_to_all | solution.py:88
  288.0 11.9 %all-to-all-start.6 = ((f32[16,1,192]{2,1,0:T(1,128)}), f32[16,1,192]{2,1,0:T(1,128)S(1)}, u32[]{:S(2)}, u32[]{:S(2)}) async-start(f32[16,1,192]{2,1,0:T(1,128)} %reshape.106), calls=%async_computation.6 | async-start | bytes 32768 | tf_op jit(solution)/shard_map/all_to_all | solution.py:80
  300.0 49.2 %all-to-all-start.7 = ((bf16[16,32,6,128]{3,0,2,1:T(8,128)(2,1)}), bf16[16,32,6,128]{3,0,2,1:T(8,128)(2,1)S(1)}, u32[]{:S(2)}, u32[]{:S(2)}) async-start(bf16[16,32,6,128]{3,0,2,1:T(8,128)(2,1)} %copy.56), calls=%async_computation.7 | async-start | bytes 1572864 | tf_op jit(solution)/shard_map/all_to_all | solution.py:73
  349.1 11.0 %all-to-all-start.4 = ((f32[16,1,192]{2,1,0:T(1,128)}), f32[16,1,192]{2,1,0:T(1,128)S(1)}, u32[]{:S(2)}, u32[]{:S(2)}) async-start(f32[16,1,192]{2,1,0:T(1,128)} %reshape.108), calls=%async_computation.4 | async-start | bytes 32768 | tf_op jit(solution)/shard_map/all_to_all | solution.py:87
  360.2 20.3 %all-to-all-start.8 = ((bf16[16,1,6,4096]{3,2,1,0:T(8,128)(2,1)}), bf16[16,1,6,4096]{3,2,1,0:T(8,128)(2,1)}, u32[]{:S(2)}, u32[]{:S(2)}) async-start(bf16[16,1,6,4096]{3,2,1,0:T(8,128)(2,1)} %reshape.103), calls=%async_computation.8 | async-start | bytes 2097152 | tf_op jit(solution)/shard_map/all_to_all | solution.py:72
where the time goes:
time: 385 us; the launch traced here: 384 us
  waiting for transfers between devices  239 us (62%)
  starting transfers between devices  48.7 us (13%)
  blocking collectives  27.6 us (7%)
  matrix products  26.2 us (7%)
  local copies, waits for them, and re-layouts  24.8 us (6%)
  other arithmetic  15.9 us (4%)
    all_to_all x1, waiting for transfers between devices, local(): lax.all_to_all(key, 'seq', split_axis=1, concat_axis=0, tiled=True)  54.2 us
    all_to_all x1, waiting for transfers between devices, local(): lax.all_to_all(value, 'seq', split_axis=1, concat_axis=0, tiled=True)  53.9 us
    all_to_all x1, waiting for transfers between devices, local(): lax.all_to_all(mixed, 'seq', split_axis=1, concat_axis=3, tiled=True)  43.6 us
    all_to_all x1, waiting for transfers between devices, local(): lax.all_to_all(gathered, 'seq', split_axis=1, concat_axis=0, tiled=True)  42.6 us
    all_gather x1, blocking collectives, local(): gathered = lax.all_gather(chosen, 'blk', axis=0, tiled=True)  27.6 us
    all_to_all x1, waiting for transfers between devices, local(): lax.all_to_all(top, 'seq', split_axis=1, concat_axis=3, tiled=True)  14.6 us
    all_to_all x1, waiting for transfers between devices, local(): lax.all_to_all(total, 'seq', split_axis=1, concat_axis=3, tiled=True)  13.6 us
    dot_general x6, matrix products, one_block(): jnp.einsum('rhd,khd->hrk', block, keys, preferred_element_type=jnp.float32)  13.4 us
  transfers between devices with their start and end apart: 9, of which 9 were waited for; matrix products, arithmetic and copies ran while one was open for 6% of the time, Pallas kernels for 0%

commit v1 on v0

--- a/solution.py
+++ b/solution.py
@@ -61,7 +61,12 @@
     )
     keys = keys.reshape(-1, per_dev, HD)
     values = values.reshape(-1, per_dev, HD)
-    gathered = lax.all_gather(chosen, "blk", axis=0, tiled=True)
+    ring = [chosen]
+    for hop in range(15):
+        ring.append(lax.ppermute(ring[-1], "blk", [(dev, (dev + 1) % 16) for dev in range(16)]))
+    gathered = jnp.roll(
+        jnp.concatenate(ring[::-1], axis=0), (lax.axis_index("blk") + 1) * ring[0].shape[0], axis=0
+    )
     spread = lax.all_to_all(gathered, "seq", split_axis=1, concat_axis=0, tiled=True)
     queries = spread.reshape(seq_size, blk_size, slots, head_width).transpose(1, 0, 2, 3)
     queries = queries.reshape(-1, per_dev, HD)

time: 385 us -> 508 us (1.32)
  waiting for transfers between devices: 239 us -> 352 us
  starting transfers between devices: 48.7 us -> 79.1 us
  blocking collectives: 27.6 us -> 0 us
  local copies, waits for them, and re-layouts: 24.8 us -> 31.1 us
    ppermute x0 -> x15, waiting for transfers between devices: none -> 113 us  [local(): lax.ppermute(ring[-1], 'blk', [(dev, (dev + 1) % 16) for dev in range(16)])]
    ppermute x0 -> x15, starting transfers between devices: none -> 30.2 us  [local(): lax.ppermute(ring[-1], 'blk', [(dev, (dev + 1) % 16) for dev in range(16)])]
    all_gather x1 -> x0, blocking collectives: 27.6 us -> none  [local(): gathered = lax.all_gather(chosen, 'blk', axis=0, tiled=True)]
    concatenate x0 -> x1, local copies, waits for them, and re-layouts: none -> 7.35 us  [local(): jnp.roll(jnp.concatenate(ring[::-1], axis=0), (lax.axis_index('blk') + 1)...]
  transfers between devices with their start and end apart: 9 -> 24, of which waited for: 9 -> 24; matrix products, arithmetic and copies ran while one was open for 6% -> 4% of each run, Pallas kernels for 0% -> 0%
where the time goes in v1:
time: 508 us; the launch traced here: 506 us
  waiting for transfers between devices  352 us (69%)
  starting transfers between devices  79.1 us (16%)
  local copies, waits for them, and re-layouts  31.1 us (6%)
  matrix products  26.3 us (5%)
  other arithmetic  16.1 us (3%)
    ppermute x15, waiting for transfers between devices, local(): lax.ppermute(ring[-1], 'blk', [(dev, (dev + 1) % 16) for dev in range(16)])  113 us
    all_to_all x1, waiting for transfers between devices, local(): lax.all_to_all(key, 'seq', split_axis=1, concat_axis=0, tiled=True)  54.2 us
    all_to_all x1, waiting for transfers between devices, local(): lax.all_to_all(value, 'seq', split_axis=1, concat_axis=0, tiled=True)  54 us
    all_to_all x1, waiting for transfers between devices, local(): lax.all_to_all(mixed, 'seq', split_axis=1, concat_axis=3, tiled=True)  43.6 us
    all_to_all x1, waiting for transfers between devices, local(): lax.all_to_all(gathered, 'seq', split_axis=1, concat_axis=0, tiled=True)  42.6 us
    ppermute x15, starting transfers between devices, local(): lax.ppermute(ring[-1], 'blk', [(dev, (dev + 1) % 16) for dev in range(16)])  30.2 us
    all_to_all x1, waiting for transfers between devices, local(): lax.all_to_all(top, 'seq', split_axis=1, concat_axis=3, tiled=True)  14.6 us
    all_to_all x1, waiting for transfers between devices, local(): lax.all_to_all(total, 'seq', split_axis=1, concat_axis=3, tiled=True)  13.5 us
  transfers between devices with their start and end apart: 24, of which 24 were waited for; matrix products, arithmetic and copies ran while one was open for 4% of the time, Pallas kernels for 0%

profile of v1, /device:TPU:8, one launch (start us, length us, event | category | flops | bytes accessed | tf_op | source)
XLA Modules:
  0.0 506.1 jit_solution(5520974722186091450)
XLA Ops:
  13.7 7.6 %collective-permute-done.1 = bf16[6,4096]{1,0:T(8,128)(2,1)S(1)} collective-permute-done((bf16[6,4096]{1,0:T(8,128)(2,1)S(1)}, bf16[6,4096]{1,0:T(8,128)(2,1)S(1)}, u32[]{:S(2)}, u32[]{:S(2)}) %collective-permute-start.1) | collective-permute-done | bytes 49184 | tf_op jit(solution)/shard_map/ppermute | solution.py:66
  23.2 8.2 %collective-permute-done.2 = bf16[6,4096]{1,0:T(8,128)(2,1)S(1)} collective-permute-done((bf16[6,4096]{1,0:T(8,128)(2,1)S(1)}, bf16[6,4096]{1,0:T(8,128)(2,1)S(1)}, u32[]{:S(2)}, u32[]{:S(2)}) %collective-permute-start.2) | collective-permute-done | bytes 49184 | tf_op jit(solution)/shard_map/ppermute | solution.py:66
  42.5 7.6 %collective-permute-done.4 = bf16[6,4096]{1,0:T(8,128)(2,1)S(1)} collective-permute-done((bf16[6,4096]{1,0:T(8,128)(2,1)S(1)}, bf16[6,4096]{1,0:T(8,128)(2,1)S(1)}, u32[]{:S(2)}, u32[]{:S(2)}) %collective-permute-start.4) | collective-permute-done | bytes 49184 | tf_op jit(solution)/shard_map/ppermute | solution.py:66
  52.0 7.6 %collective-permute-done.5 = bf16[6,4096]{1,0:T(8,128)(2,1)S(1)} collective-permute-done((bf16[6,4096]{1,0:T(8,128)(2,1)S(1)}, bf16[6,4096]{1,0:T(8,128)(2,1)S(1)}, u32[]{:S(2)}, u32[]{:S(2)}) %collective-permute-start.5) | collective-permute-done | bytes 49184 | tf_op jit(solution)/shard_map/ppermute | solution.py:66
  61.4 7.6 %collective-permute-done.6 = bf16[6,4096]{1,0:T(8,128)(2,1)S(1)} collective-permute-done((bf16[6,4096]{1,0:T(8,128)(2,1)S(1)}, bf16[6,4096]{1,0:T(8,128)(2,1)S(1)}, u32[]{:S(2)}, u32[]{:S(2)}) %collective-permute-start.6) | collective-permute-done | bytes 49184 | tf_op jit(solution)/shard_map/ppermute | solution.py:66
  70.9 7.6 %collective-permute-done.7 = bf16[6,4096]{1,0:T(8,128)(2,1)S(1)} collective-permute-done((bf16[6,4096]{1,0:T(8,128)(2,1)S(1)}, bf16[6,4096]{1,0:T(8,128)(2,1)S(1)}, u32[]{:S(2)}, u32[]{:S(2)}) %collective-permute-start.7) | collective-permute-done | bytes 49184 | tf_op jit(solution)/shard_map/ppermute | solution.py:66
  80.4 7.6 %collective-permute-done.8 = bf16[6,4096]{1,0:T(8,128)(2,1)S(1)} collective-permute-done((bf16[6,4096]{1,0:T(8,128)(2,1)S(1)}, bf16[6,4096]{1,0:T(8,128)(2,1)S(1)}, u32[]{:S(2)}, u32[]{:S(2)}) %collective-permute-start.8) | collective-permute-done | bytes 49184 | tf_op jit(solution)/shard_map/ppermute | solution.py:66
  89.8 7.8 %collective-permute-done.9 = bf16[6,4096]{1,0:T(8,128)(2,1)S(1)} collective-permute-done((bf16[6,4096]{1,0:T(8,128)(2,1)S(1)}, bf16[6,4096]{1,0:T(8,128)(2,1)S(1)}, u32[]{:S(2)}, u32[]{:S(2)}) %collective-permute-start.9) | collective-permute-done | bytes 49184 | tf_op jit(solution)/shard_map/ppermute | solution.py:66
  99.6 7.9 %collective-permute-done.10 = bf16[6,4096]{1,0:T(8,128)(2,1)S(1)} collective-permute-done((bf16[6,4096]{1,0:T(8,128)(2,1)S(1)}, bf16[6,4096]{1,0:T(8,128)(2,1)S(1)}, u32[]{:S(2)}, u32[]{:S(2)}) %collective-permute-start.10) | collective-permute-done | bytes 49184 | tf_op jit(solution)/shard_map/ppermute | solution.py:66
  109.4 7.4 %collective-permute-done.11 = bf16[6,4096]{1,0:T(8,128)(2,1)S(1)} collective-permute-done((bf16[6,4096]{1,0:T(8,128)(2,1)S(1)}, bf16[6,4096]{1,0:T(8,128)(2,1)S(1)}, u32[]{:S(2)}, u32[]{:S(2)}) %collective-permute-start.11) | collective-permute-done | bytes 49184 | tf_op jit(solution)/shard_map/ppermute | solution.py:66
  118.7 7.6 %collective-permute-done.12 = bf16[6,4096]{1,0:T(8,128)(2,1)S(1)} collective-permute-done((bf16[6,4096]{1,0:T(8,128)(2,1)S(1)}, bf16[6,4096]{1,0:T(8,128)(2,1)S(1)}, u32[]{:S(2)}, u32[]{:S(2)}) %collective-permute-start.12) | collective-permute-done | bytes 49184 | tf_op jit(solution)/shard_map/ppermute | solution.py:66
  128.2 7.6 %collective-permute-done.13 = bf16[6,4096]{1,0:T(8,128)(2,1)S(1)} collective-permute-done((bf16[6,4096]{1,0:T(8,128)(2,1)S(1)}, bf16[6,4096]{1,0:T(8,128)(2,1)S(1)}, u32[]{:S(2)}, u32[]{:S(2)}) %collective-permute-start.13) | collective-permute-done | bytes 49184 | tf_op jit(solution)/shard_map/ppermute | solution.py:66
  137.7 7.6 %collective-permute-done.14 = bf16[6,4096]{1,0:T(8,128)(2,1)} collective-permute-done((bf16[6,4096]{1,0:T(8,128)(2,1)S(1)}, bf16[6,4096]{1,0:T(8,128)(2,1)}, u32[]{:S(2)}, u32[]{:S(2)}) %collective-permute-start.14) | collective-permute-done | bytes 49184 | tf_op jit(solution)/shard_map/ppermute | solution.py:66
  145.3 7.3 %concatenate.6 = bf16[192,4096]{1,0:T(8,128)(2,1)S(1)} concatenate(bf16[6,4096]{1,0:T(8,128)(2,1)} %collective-permute-done.14, bf16[6,4096]{1,0:T(8,128)(2,1)} %copy-done.1, bf16[6,4096]{1,0:T(8,128)(2,1)S(1)} %collective-permute-done.12, bf16[6,4096]{1,0:T(8,128)(2,1)S(1)} %collective-permute-done.11, bf16[6,4096]{1,0:T(8,128)(2,1)S(1)} %collective-permute-done.10, ...), dimensions={0} | concatenate | bytes 3145728 | tf_op jit(solution)/shard_map/jit(_roll_dynamic)/concatenate | solution.py:67
  153.8 9.6 %all-to-all-start = ((bf16[96,32,128]{2,0,1:T(8,128)(2,1)}), bf16[96,32,128]{2,0,1:T(8,128)(2,1)S(1)}, u32[]{:S(2)}, u32[]{:S(2)}) async-start(bf16[96,32,128]{2,0,1:T(8,128)(2,1)} %copy_bitcast_fusion), calls=%async_computation | async-start | bytes 1572864 | tf_op jit(solution)/shard_map/all_to_all | solution.py:70
  165.7 42.6 %all-to-all-done = bf16[96,32,128]{2,0,1:T(8,128)(2,1)S(1)} async-done(((bf16[96,32,128]{2,0,1:T(8,128)(2,1)}), bf16[96,32,128]{2,0,1:T(8,128)(2,1)S(1)}, u32[]{:S(2)}, u32[]{:S(2)}) %all-to-all-start) | async-done | bytes 786464 | tf_op jit(solution)/shard_map/all_to_all | solution.py:70
  214.5 54.2 %all-to-all-done.1 = bf16[128,32,128]{0,2,1:T(8,128)(2,1)S(1)} async-done(((bf16[128,32,128]{0,2,1:T(8,128)(2,1)}), bf16[128,32,128]{0,2,1:T(8,128)(2,1)S(1)}, u32[]{:S(2)}, u32[]{:S(2)}) %all-to-all-start.1) | async-done | bytes 1048608 | tf_op jit(solution)/shard_map/all_to_all | solution.py:59
  276.0 54.0 %all-to-all-done.2 = bf16[128,32,128]{0,2,1:T(8,128)(2,1)} async-done(((bf16[128,32,128]{0,2,1:T(8,128)(2,1)}), bf16[128,32,128]{0,2,1:T(8,128)(2,1)}, u32[]{:S(2)}, u32[]{:S(2)}) %all-to-all-start.2) | async-done | bytes 1048608 | tf_op jit(solution)/shard_map/all_to_all | solution.py:60
  331.5 35.4 %while.14 = (s32[]{:T(128)}, bf16[6,512,1,128]{3,1,2,0:T(8,128)(2,1)}, f32[6,512,1]{1,2,0:T(1,128)S(1)}, f32[6,512,1]{1,2,0:T(1,128)S(1)}, bf16[6,512,1,128]{3,1...) while((s32[]{:T(128)}, ...), condition=%wide.region_3.4_spmd, body=%wide.region_0.3_spmd.sunk | while | flops 1090649088 | bytes 27544664 | solution.py:35
  373.3 14.6 %all-to-all-done.5 = f32[16,32,6,1]{0,3,2,1:T(1,128)S(1)} async-done(((f32[16,32,6,1]{0,3,2,1:T(1,128)}), f32[16,32,6,1]{0,3,2,1:T(1,128)S(1)}, u32[]{:S(2)}, u32[]{:S(2)}) %all-to-all-start.5) | async-done | bytes 12320 | tf_op jit(solution)/shard_map/all_to_all | solution.py:86
  394.0 13.5 %all-to-all-done.3 = f32[16,32,6,1]{0,3,2,1:T(1,128)S(1)} async-done(((f32[16,32,6,1]{0,3,2,1:T(1,128)}), f32[16,32,6,1]{0,3,2,1:T(1,128)S(1)}, u32[]{:S(2)}, u32[]{:S(2)}) %all-to-all-start.3) | async-done | bytes 12320 | tf_op jit(solution)/shard_map/all_to_all | solution.py:93
  407.5 8.6 %all-to-all-start.6 = ((f32[16,1,192]{2,1,0:T(1,128)}), f32[16,1,192]{2,1,0:T(1,128)S(1)}, u32[]{:S(2)}, u32[]{:S(2)}) async-start(f32[16,1,192]{2,1,0:T(1,128)} %reshape.102), calls=%async_computation.6 | async-start | bytes 32768 | tf_op jit(solution)/shard_map/all_to_all | solution.py:85
  428.0 43.6 %all-to-all-done.7 = bf16[16,32,6,128]{3,0,2,1:T(8,128)(2,1)S(1)} async-done(((bf16[16,32,6,128]{3,0,2,1:T(8,128)(2,1)}), bf16[16,32,6,128]{3,0,2,1:T(8,128)(2,1)S(1)}, u32[]{:S(2)}, u32[]{:S(2)}) %all-to-all-start.7) | async-done | bytes 786464 | tf_op jit(solution)/shard_map/all_to_all | solution.py:78
  493.5 9.4 %all-to-all-done.8 = bf16[16,1,6,4096]{3,2,1,0:T(8,128)(2,1)} async-done(((bf16[16,1,6,4096]{3,2,1,0:T(8,128)(2,1)}), bf16[16,1,6,4096]{3,2,1,0:T(8,128)(2,1)}, u32[]{:S(2)}, u32[]{:S(2)}) %all-to-all-start.8) | async-done | bytes 786464 | tf_op jit(solution)/shard_map/all_to_all | solution.py:77
  (100 shorter events, 147.4 us)
Async XLA Ops:
  1.8 10.0 %collective-permute-start = (bf16[6,4096]{1,0:T(8,128)(2,1)S(1)}, bf16[6,4096]{1,0:T(8,128)(2,1)S(1)}, u32[]{:S(2)}, u32[]{:S(2)}) collective-permute-start(bf16[6,4096]{1,0:T(8,128)(2,1)S(1)} %gather_fusion), channel_id=1, source_target_pairs={{0,1},{1,2},{2,3},{3,4},{4,5},{5,6},{6,7},{7,8},{8,9},{9,10},{10,1... | collective-permute-start | bytes 147464 | tf_op jit(solution)/shard_map/ppermute | solution.py:66
  11.8 9.5 %collective-permute-start.1 = (bf16[6,4096]{1,0:T(8,128)(2,1)S(1)}, bf16[6,4096]{1,0:T(8,128)(2,1)S(1)}, u32[]{:S(2)}, u32[]{:S(2)}) collective-permute-start(bf16[6,4096]{1,0:T(8,128)(2,1)S(1)} %collective-permute-done), channel_id=1, source_target_pairs={{0,1},{1,2},{2,3},{3,4},{4,5},{5,6},{6,7},{7,8},{8,9},{9,10},{10,1... | collective-permute-start | bytes 147464 | tf_op jit(solution)/shard_map/ppermute | solution.py:66
  21.3 10.1 %collective-permute-start.2 = (bf16[6,4096]{1,0:T(8,128)(2,1)S(1)}, bf16[6,4096]{1,0:T(8,128)(2,1)S(1)}, u32[]{:S(2)}, u32[]{:S(2)}) collective-permute-start(bf16[6,4096]{1,0:T(8,128)(2,1)S(1)} %collective-permute-done.1), channel_id=1, source_target_pairs={{0,1},{1,2},{2,3},{3,4},{4,5},{5,6},{6,7},{7,8},{8,9},{9,10},{10,1... | collective-permute-start | bytes 147464 | tf_op jit(solution)/shard_map/ppermute | solution.py:66
  31.4 9.2 %collective-permute-start.3 = (bf16[6,4096]{1,0:T(8,128)(2,1)S(1)}, bf16[6,4096]{1,0:T(8,128)(2,1)S(1)}, u32[]{:S(2)}, u32[]{:S(2)}) collective-permute-start(bf16[6,4096]{1,0:T(8,128)(2,1)S(1)} %collective-permute-done.2), channel_id=1, source_target_pairs={{0,1},{1,2},{2,3},{3,4},{4,5},{5,6},{6,7},{7,8},{8,9},{9,10},{10,1... | collective-permute-start | bytes 147464 | tf_op jit(solution)/shard_map/ppermute | solution.py:66
  40.6 9.5 %collective-permute-start.4 = (bf16[6,4096]{1,0:T(8,128)(2,1)S(1)}, bf16[6,4096]{1,0:T(8,128)(2,1)S(1)}, u32[]{:S(2)}, u32[]{:S(2)}) collective-permute-start(bf16[6,4096]{1,0:T(8,128)(2,1)S(1)} %collective-permute-done.3), channel_id=1, source_target_pairs={{0,1},{1,2},{2,3},{3,4},{4,5},{5,6},{6,7},{7,8},{8,9},{9,10},{10,1... | collective-permute-start | bytes 147464 | tf_op jit(solution)/shard_map/ppermute | solution.py:66
  50.0 9.5 %collective-permute-start.5 = (bf16[6,4096]{1,0:T(8,128)(2,1)S(1)}, bf16[6,4096]{1,0:T(8,128)(2,1)S(1)}, u32[]{:S(2)}, u32[]{:S(2)}) collective-permute-start(bf16[6,4096]{1,0:T(8,128)(2,1)S(1)} %collective-permute-done.4), channel_id=1, source_target_pairs={{0,1},{1,2},{2,3},{3,4},{4,5},{5,6},{6,7},{7,8},{8,9},{9,10},{10,1... | collective-permute-start | bytes 147464 | tf_op jit(solution)/shard_map/ppermute | solution.py:66
  59.5 9.5 %collective-permute-start.6 = (bf16[6,4096]{1,0:T(8,128)(2,1)S(1)}, bf16[6,4096]{1,0:T(8,128)(2,1)S(1)}, u32[]{:S(2)}, u32[]{:S(2)}) collective-permute-start(bf16[6,4096]{1,0:T(8,128)(2,1)S(1)} %collective-permute-done.5), channel_id=1, source_target_pairs={{0,1},{1,2},{2,3},{3,4},{4,5},{5,6},{6,7},{7,8},{8,9},{9,10},{10,1... | collective-permute-start | bytes 147464 | tf_op jit(solution)/shard_map/ppermute | solution.py:66
  69.0 9.5 %collective-permute-start.7 = (bf16[6,4096]{1,0:T(8,128)(2,1)S(1)}, bf16[6,4096]{1,0:T(8,128)(2,1)S(1)}, u32[]{:S(2)}, u32[]{:S(2)}) collective-permute-start(bf16[6,4096]{1,0:T(8,128)(2,1)S(1)} %collective-permute-done.6), channel_id=1, source_target_pairs={{0,1},{1,2},{2,3},{3,4},{4,5},{5,6},{6,7},{7,8},{8,9},{9,10},{10,1... | collective-permute-start | bytes 147464 | tf_op jit(solution)/shard_map/ppermute | solution.py:66
  78.4 9.5 %collective-permute-start.8 = (bf16[6,4096]{1,0:T(8,128)(2,1)S(1)}, bf16[6,4096]{1,0:T(8,128)(2,1)S(1)}, u32[]{:S(2)}, u32[]{:S(2)}) collective-permute-start(bf16[6,4096]{1,0:T(8,128)(2,1)S(1)} %collective-permute-done.7), channel_id=1, source_target_pairs={{0,1},{1,2},{2,3},{3,4},{4,5},{5,6},{6,7},{7,8},{8,9},{9,10},{10,1... | collective-permute-start | bytes 147464 | tf_op jit(solution)/shard_map/ppermute | solution.py:66
  87.9 9.7 %collective-permute-start.9 = (bf16[6,4096]{1,0:T(8,128)(2,1)S(1)}, bf16[6,4096]{1,0:T(8,128)(2,1)S(1)}, u32[]{:S(2)}, u32[]{:S(2)}) collective-permute-start(bf16[6,4096]{1,0:T(8,128)(2,1)S(1)} %collective-permute-done.8), channel_id=1, source_target_pairs={{0,1},{1,2},{2,3},{3,4},{4,5},{5,6},{6,7},{7,8},{8,9},{9,10},{10,1... | collective-permute-start | bytes 147464 | tf_op jit(solution)/shard_map/ppermute | solution.py:66
  97.6 9.8 %collective-permute-start.10 = (bf16[6,4096]{1,0:T(8,128)(2,1)S(1)}, bf16[6,4096]{1,0:T(8,128)(2,1)S(1)}, u32[]{:S(2)}, u32[]{:S(2)}) collective-permute-start(bf16[6,4096]{1,0:T(8,128)(2,1)S(1)} %collective-permute-done.9), channel_id=1, source_target_pairs={{0,1},{1,2},{2,3},{3,4},{4,5},{5,6},{6,7},{7,8},{8,9},{9,10},{10,1... | collective-permute-start | bytes 147464 | tf_op jit(solution)/shard_map/ppermute | solution.py:66
  107.4 9.3 %collective-permute-start.11 = (bf16[6,4096]{1,0:T(8,128)(2,1)S(1)}, bf16[6,4096]{1,0:T(8,128)(2,1)S(1)}, u32[]{:S(2)}, u32[]{:S(2)}) collective-permute-start(bf16[6,4096]{1,0:T(8,128)(2,1)S(1)} %collective-permute-done.10), channel_id=1, source_target_pairs={{0,1},{1,2},{2,3},{3,4},{4,5},{5,6},{6,7},{7,8},{8,9},{9,10},{10,1... | collective-permute-start | bytes 147464 | tf_op jit(solution)/shard_map/ppermute | solution.py:66
  116.8 9.5 %collective-permute-start.12 = (bf16[6,4096]{1,0:T(8,128)(2,1)S(1)}, bf16[6,4096]{1,0:T(8,128)(2,1)S(1)}, u32[]{:S(2)}, u32[]{:S(2)}) collective-permute-start(bf16[6,4096]{1,0:T(8,128)(2,1)S(1)} %collective-permute-done.11), channel_id=1, source_target_pairs={{0,1},{1,2},{2,3},{3,4},{4,5},{5,6},{6,7},{7,8},{8,9},{9,10},{10,1... | collective-permute-start | bytes 147464 | tf_op jit(solution)/shard_map/ppermute | solution.py:66
  126.3 9.5 %collective-permute-start.13 = (bf16[6,4096]{1,0:T(8,128)(2,1)S(1)}, bf16[6,4096]{1,0:T(8,128)(2,1)S(1)}, u32[]{:S(2)}, u32[]{:S(2)}) collective-permute-start(bf16[6,4096]{1,0:T(8,128)(2,1)S(1)} %collective-permute-done.12), channel_id=1, source_target_pairs={{0,1},{1,2},{2,3},{3,4},{4,5},{5,6},{6,7},{7,8},{8,9},{9,10},{10,1... | collective-permute-start | bytes 147464 | tf_op jit(solution)/shard_map/ppermute | solution.py:66
  135.7 9.6 %collective-permute-start.14 = (bf16[6,4096]{1,0:T(8,128)(2,1)S(1)}, bf16[6,4096]{1,0:T(8,128)(2,1)}, u32[]{:S(2)}, u32[]{:S(2)}) collective-permute-start(bf16[6,4096]{1,0:T(8,128)(2,1)S(1)} %collective-permute-done.13), channel_id=1, source_target_pairs={{0,1},{1,2},{2,3},{3,4},{4,5},{5,6},{6,7},{7,8},{8,9},{9,10},{10,1... | collective-permute-start | bytes 147464 | tf_op jit(solution)/shard_map/ppermute | solution.py:66
  153.8 54.5 %all-to-all-start = ((bf16[96,32,128]{2,0,1:T(8,128)(2,1)}), bf16[96,32,128]{2,0,1:T(8,128)(2,1)S(1)}, u32[]{:S(2)}, u32[]{:S(2)}) async-start(bf16[96,32,128]{2,0,1:T(8,128)(2,1)} %copy_bitcast_fusion), calls=%async_computation | async-start | bytes 1572864 | tf_op jit(solution)/shard_map/all_to_all | solution.py:70
  208.3 60.4 %all-to-all-start.1 = ((bf16[128,32,128]{0,2,1:T(8,128)(2,1)}), bf16[128,32,128]{0,2,1:T(8,128)(2,1)S(1)}, u32[]{:S(2)}, u32[]{:S(2)}) async-start(bf16[128,32,128]{0,2,1:T(8,128)(2,1)} %bitcast.16), calls=%async_computation.1 | async-start | bytes 2097152 | tf_op jit(solution)/shard_map/all_to_all | solution.py:59
  268.7 61.2 %all-to-all-start.2 = ((bf16[128,32,128]{0,2,1:T(8,128)(2,1)}), bf16[128,32,128]{0,2,1:T(8,128)(2,1)}, u32[]{:S(2)}, u32[]{:S(2)}) async-start(bf16[128,32,128]{0,2,1:T(8,128)(2,1)} %bitcast.19), calls=%async_computation.2 | async-start | bytes 2097152 | tf_op jit(solution)/shard_map/all_to_all | solution.py:60
  368.1 19.8 %all-to-all-start.5 = ((f32[16,32,6,1]{0,3,2,1:T(1,128)}), f32[16,32,6,1]{0,3,2,1:T(1,128)S(1)}, u32[]{:S(2)}, u32[]{:S(2)}) async-start(f32[16,32,6,1]{0,3,2,1:T(1,128)} %copy.51), calls=%async_computation.5 | async-start | bytes 196608 | tf_op jit(solution)/shard_map/all_to_all | solution.py:86
  387.9 19.6 %all-to-all-start.3 = ((f32[16,32,6,1]{0,3,2,1:T(1,128)}), f32[16,32,6,1]{0,3,2,1:T(1,128)S(1)}, u32[]{:S(2)}, u32[]{:S(2)}) async-start(f32[16,32,6,1]{0,3,2,1:T(1,128)} %copy.47), calls=%async_computation.3 | async-start | bytes 196608 | tf_op jit(solution)/shard_map/all_to_all | solution.py:93
  407.5 14.9 %all-to-all-start.6 = ((f32[16,1,192]{2,1,0:T(1,128)}), f32[16,1,192]{2,1,0:T(1,128)S(1)}, u32[]{:S(2)}, u32[]{:S(2)}) async-start(f32[16,1,192]{2,1,0:T(1,128)} %reshape.102), calls=%async_computation.6 | async-start | bytes 32768 | tf_op jit(solution)/shard_map/all_to_all | solution.py:85
  422.4 49.2 %all-to-all-start.7 = ((bf16[16,32,6,128]{3,0,2,1:T(8,128)(2,1)}), bf16[16,32,6,128]{3,0,2,1:T(8,128)(2,1)S(1)}, u32[]{:S(2)}, u32[]{:S(2)}) async-start(bf16[16,32,6,128]{3,0,2,1:T(8,128)(2,1)} %copy.55), calls=%async_computation.7 | async-start | bytes 1572864 | tf_op jit(solution)/shard_map/all_to_all | solution.py:78
  471.6 11.0 %all-to-all-start.4 = ((f32[16,1,192]{2,1,0:T(1,128)}), f32[16,1,192]{2,1,0:T(1,128)S(1)}, u32[]{:S(2)}, u32[]{:S(2)}) async-start(f32[16,1,192]{2,1,0:T(1,128)} %reshape.104), calls=%async_computation.4 | async-start | bytes 32768 | tf_op jit(solution)/shard_map/all_to_all | solution.py:92
  482.7 20.3 %all-to-all-start.8 = ((bf16[16,1,6,4096]{3,2,1,0:T(8,128)(2,1)}), bf16[16,1,6,4096]{3,2,1,0:T(8,128)(2,1)}, u32[]{:S(2)}, u32[]{:S(2)}) async-start(bf16[16,1,6,4096]{3,2,1,0:T(8,128)(2,1)} %reshape.99), calls=%async_computation.8 | async-start | bytes 2097152 | tf_op jit(solution)/shard_map/all_to_all | solution.py:77
  (2 other events, 3.2 us)
